TPU v7x, 512 devices: a whole 4x8x8 slice. The times are simulated.
512 devices in a mesh: trade: 32 (over x, y), path: 16 (over z, core).
Axes of the slice: x: 4, y: 8, z: 8, core: 2. Of those that a mesh axis runs over, the one named last changes fastest.
Arguments:
- coef: bfloat16 [2, 64, 16384], P(None, None, 'trade'), may hold values from -0.75 to 0.75
- membership: int32 [16384], P('trade'), may hold values from 0 to 4095
- trade_type: int32 [16384], P('trade'), may hold values from 0 to 7
- type_notional: float32 [8], replicated, may hold values from 0.5 to 4
- basis_start: bfloat16 [64, 1024], P(None, 'path'), may hold values from -6 to 6
- shocks: bfloat16 [64, 1024], P(None, 'path'), may hold values from -6 to 6
- basis_map: bfloat16 [64, 64], replicated, may hold values from -0.75 to 0.75
- credit_weight: bfloat16 [2, 1024, 4096], P(None, 'path'), may hold values from 0.5 to 8
Outputs:
- exposure: float32 [2, 4096], P(None, 'trade')
- coef_grad: float32 [2, 64, 16384], P(None, None, 'trade')
- basis_grad: float32 [64, 1024], P(None, 'path')
All inputs are finite; a program needn't handle non-finite values.
Results may differ from a plain program's by a relative error of at most 0.0029.
Values may be sent and summed in bfloat16 or wider, within the bound.
A program may use at most 64 MiB of HBM per device.

v0:
```python
import math

import jax
import jax.numpy as jnp
from jax import lax
from jax.sharding import PartitionSpec as P


def shards(
    coef, membership, trade_type, type_notional, basis_start, shocks, basis_map, credit_weight
):
    trade_rows = coef.shape[2]
    path_rows = basis_start.shape[1]
    set_count = credit_weight.shape[2]
    trade_size = lax.axis_size("trade")
    path_size = lax.axis_size("path")
    share = set_count // trade_size
    owner = lax.axis_index("trade")
    block = min(256, trade_rows)
    blocks = trade_rows // block
    kinds = lax.broadcasted_iota(jnp.int32, (trade_rows, type_notional.shape[0]), 1)
    notional = jnp.sum(jnp.where(trade_type[:, None] == kinds, type_notional[None, :], 0.0), axis=1)
    pre = lax.dot_general(
        basis_map, basis_start, (((0,), (0,)), ((), ())), preferred_element_type=jnp.float32
    )
    later = jnp.tanh(pre + shocks.astype(jnp.float32)).astype(jnp.bfloat16)
    bases = (basis_start, later)
    values = tuple(
        (
            (
                lax.dot_general(
                    bases[step],
                    coef[step],
                    (((0,), (0,)), ((), ())),
                    preferred_element_type=jnp.float32,
                )
                * notional[None, :]
            ).astype(jnp.bfloat16)
            for step in range(2)
        )
    )
    set_ids = lax.broadcasted_iota(jnp.int32, (block, set_count), 1)

    def forward(index, totals):
        start = index * block
        members = lax.dynamic_slice_in_dim(membership, start, block)
        onehot = (members[:, None] == set_ids).astype(jnp.bfloat16)
        return tuple(
            (
                totals[step]
                + jnp.dot(
                    lax.dynamic_slice_in_dim(values[step], start, block, 1),
                    onehot,
                    preferred_element_type=jnp.float32,
                )
                for step in range(2)
            )
        )

    empty_sets = jnp.zeros((path_rows, set_count), jnp.float32)
    totals = lax.fori_loop(0, blocks, forward, (empty_sets, empty_sets))
    empty_trades = jnp.zeros((path_rows, trade_rows), jnp.float32)
    full = lax.psum((totals[0], totals[1]), "trade")
    set_adj = tuple(
        (
            (credit_weight[step].astype(jnp.float32) * jax.nn.sigmoid(full[step])).astype(
                jnp.bfloat16
            )
            for step in range(2)
        )
    )
    own = tuple(
        (lax.dynamic_slice_in_dim(full[step], owner * share, share, 1) for step in range(2))
    )

    def backward(index, raws):
        start = index * block
        members = lax.dynamic_slice_in_dim(membership, start, block)
        onehot = (members[:, None] == set_ids).astype(jnp.bfloat16)
        return tuple(
            (
                lax.dynamic_update_slice_in_dim(
                    raws[step],
                    lax.dot_general(
                        set_adj[step],
                        onehot,
                        (((1,), (1,)), ((), ())),
                        preferred_element_type=jnp.float32,
                    ),
                    start,
                    1,
                )
                for step in range(2)
            )
        )

    raw = lax.fori_loop(0, blocks, backward, (empty_trades, empty_trades))
    trade_adj = tuple(((raw[step] * notional[None, :]).astype(jnp.bfloat16) for step in range(2)))
    exposure_part = jnp.stack([jnp.sum(jax.nn.softplus(own[step]), axis=0) for step in range(2)])
    coef_part = jnp.stack(
        [
            jnp.dot(bases[step], trade_adj[step], preferred_element_type=jnp.float32)
            for step in range(2)
        ]
    )
    exposure_total = lax.psum(exposure_part, "path")
    coef_total = lax.psum(coef_part, "path")
    paths_all = path_rows * path_size
    exposure = exposure_total / paths_all
    coef_grad = coef_total / math.sqrt(paths_all)
    pulls = tuple(
        (
            lax.dot_general(
                coef[step],
                trade_adj[step],
                (((1,), (1,)), ((), ())),
                preferred_element_type=jnp.float32,
            )
            for step in range(2)
        )
    )
    slope = 1.0 - later.astype(jnp.float32) ** 2
    map_wide = basis_map.astype(jnp.float32)
    later_pull = lax.psum(pulls[1], "trade")
    early_pull = lax.psum(pulls[0], "trade")
    gathered = early_pull + jnp.dot(map_wide, later_pull * slope, precision=lax.Precision.HIGHEST)
    basis_grad = gathered / math.sqrt(trade_rows * trade_size)
    return (exposure, coef_grad, basis_grad)


def solution(mesh):
    placed = (
        P(None, None, "trade"),
        P("trade"),
        P("trade"),
        P(),
        P(None, "path"),
        P(None, "path"),
        P(),
        P(None, "path", None),
    )
    return jax.shard_map(
        shards,
        mesh=mesh,
        in_specs=placed,
        out_specs=(P(None, "trade"), P(None, None, "trade"), P(None, "path")),
        check_vma=False,
    )
```

profile of v0, /device:TPU:1, one launch (start us, length us, event | category | flops | bytes accessed | tf_op | source)
XLA Modules:
  0.0 455.2 jit_solution(7868984412534707398)
XLA Ops:
  7.2 0.8 select_reduce_fusion
  8.0 0.9 fusion.23
  8.9 1.0 fusion.18
  10.0 1.0 fusion.19
  11.0 5.9 %while.33 = (s32[]{:T(128)}, f32[64,4096]{1,0:T(8,128)S(1)}, f32[64,4096]{1,0:T(8,128)S(1)}, bf16[64,512]{1,0:T(8,128)(2,1)S(1)}, s32[512]{0:T(512)}, /*index=5*...) while((s32[]{:T(128)}, f32[64,4096]{1,0:T(8,128)S(1)}, ...), condition=%wide.region_2.3_spmd.clone, body=%wide.region_1.2_spmd.clone.sunk | while | flops 271581184 | bytes 4264106 | solution.py:61
  11.0 0.8 dynamic_slice.53
  11.8 1.1 convolution_add_fusion.6
  12.9 1.1 convolution_add_fusion.5
  14.0 0.8 dynamic_slice.53
  14.7 1.1 convolution_add_fusion.6
  15.8 1.1 convolution_add_fusion.5
  17.0 0.9 copy-done.1
  17.9 0.3 copy-done.2
  18.3 166.4 %all-reduce.7.cloned.1.call-done = (f32[64,4096]{1,0:T(8,128)}, f32[64,4096]{1,0:T(8,128)}) async-done(((f32[64,4096]{1,0:T(8,128)}, f32[64,4096]{1,0:T(8,128)}), (f32[64,4096]{1,0:T(8,128)}, f32[64,4096]{1,0:T(8,128)})) %all-reduce.7.cloned.1.call-update) | async-done | bytes 2097168 | tf_op jit(solution)/shard_map/psum | solution.py:63
  184.8 2.1 fusion.24
  186.9 3.8 while.32
  187.0 0.9 fusion.60
  187.9 0.9 fusion.59
  188.9 0.9 fusion.60
  189.8 0.9 fusion.59
  190.9 0.1 convolution_bitcast_fusion
  191.1 0.2 convolution_bitcast_fusion.3
  191.2 0.1 convolution_bitcast_fusion.1
  191.4 112.5 %all-reduce = (f32[64,64]{0,1:T(8,128)S(1)}, f32[64,64]{1,0:T(8,128)S(1)}) all-reduce(f32[64,64]{0,1:T(8,128)S(1)} %convolution_bitcast_fusion.4, f32[64,64]{1,0:T(8,128)S(1)} %convolution_bitcast_fusion.3), channel_id=1, replica_groups=mesh['trade'=32,'path'=16] {'trade'}, use_global_device_ids=true, to_apply=%region_11.12 | all-reduce | flops 8192 | bytes 65536 | tf_op jit(solution)/shard_map/psum | solution.py:125
  303.9 0.2 fusion.21
  304.2 0.7 copy.12
  304.9 0.7 pad_maximum_fusion
  305.6 0.8 fusion.34
  306.4 56.9 %psum.44 = f32[2,128]{1,0:T(2,128)S(1)} all-reduce(f32[2,128]{1,0:T(2,128)S(1)} %pad_maximum_fusion.1), channel_id=1, replica_groups=mesh['trade'=32,'path'=16] {'path'}, use_global_device_ids=true, to_apply=%region_7.8 | all-reduce | flops 256 | bytes 2048 | tf_op jit(solution)/shard_map/psum | solution.py:106
  363.3 0.6 broadcast_multiply_fusion.1
  363.9 82.8 %all-reduce.5.cloned.1.call-done = f32[2,64,512]{2,1,0:T(8,128)} async-done(((f32[2,64,512]{2,1,0:T(8,128)}), f32[2,64,512]{2,1,0:T(8,128)}) %all-reduce.5.cloned.1.call-update) | async-done | bytes 262160 | tf_op jit(solution)/shard_map/psum | solution.py:107
  446.7 1.7 broadcast_multiply_fusion
  (24 shorter events, 0.5 us)
Async XLA Ops:
  7.2 0.9 copy-start
  7.2 177.6 %all-reduce.7.cloned.1.call-start = ((), (), s32[]{:S(2)}) async-start(), calls=%async_computation.1 | async-start | bytes 4194304 | tf_op jit(solution)/shard_map/psum | solution.py:63
  16.9 1.0 copy-start.1
  16.9 1.3 copy-start.2
  16.9 167.8 %copy-start.3 = (bf16[2,64,4096]{2,1,0:T(8,128)(2,1)S(1)}, bf16[2,64,4096]{2,1,0:T(8,128)(2,1)}, u32[]{:S(2)}) copy-start(bf16[2,64,4096]{2,1,0:T(8,128)(2,1)} %param.19) | copy-start | bytes 3145732
  18.2 428.5 %all-reduce.5.cloned.1.call-start = ((), (), s32[]{:S(2)}) async-start(), calls=%async_computation | async-start | bytes 524288 | tf_op jit(solution)/shard_map/psum | solution.py:107
  184.8 2.2 copy-start.6
  186.9 3.9 copy-start.4
  190.8 113.2 %copy-start.5 = (bf16[64,64]{1,0:T(8,128)(2,1)S(1)}, bf16[64,64]{1,0:T(8,128)(2,1)}, u32[]{:S(2)}) copy-start(bf16[64,64]{1,0:T(8,128)(2,1)} %param.18) | copy-start | bytes 24580
Sparse Core Ops, SparseCore 0:
  18.4 166.3 all-reduce.6
  305.7 140.9 all-reduce.4
where the time goes:
time: 456 us; the launch traced here: 455 us
  waiting for transfers between devices  249 us (55%)
  blocking collectives  169 us (37%)
  between operations  14.2 us (3%)
  matrix products  11.7 us (3%)
  other arithmetic  6.7 us (1%)
    psum x1, waiting for transfers between devices, shards(): full = lax.psum((totals[0], totals[1]), 'trade')  166 us
    psum x1, blocking collectives, shards(): early_pull = lax.psum(pulls[0], 'trade')  113 us
    psum x1, waiting for transfers between devices, shards(): coef_total = lax.psum(coef_part, 'path')  82.8 us
    psum x1, blocking collectives, shards(): exposure_total = lax.psum(exposure_part, 'path')  56.9 us
  transfers between devices with their start and end apart: 2, of which 2 were waited for; matrix products, arithmetic and copies ran while one was open for 0% of the time, Pallas kernels for 0%

commit v1 on v0

v1 whole, which is shorter than its diff:
```python
import functools
import math

import jax
import jax.numpy as jnp
from jax import lax
from jax.experimental import pallas as pl
from jax.experimental.pallas import tpu as pltpu
from jax.sharding import PartitionSpec as P

MESH = pl.DeviceIdType.MESH
NT = 32
NY = 8
NP = 16
F32 = jnp.float32
BF16 = jnp.bfloat16


def dot(a, b):
    return jnp.dot(a, b, preferred_element_type=F32)


def dot_nt(a, b):
    return lax.dot_general(a, b, (((1,), (1,)), ((), ())), preferred_element_type=F32)


def split(v):
    high = v.astype(BF16)
    return high, (v - high.astype(F32)).astype(BF16)


def eye(rows, cols, shift):
    r = lax.broadcasted_iota(jnp.int32, (rows, cols), 0)
    c = lax.broadcasted_iota(jnp.int32, (rows, cols), 1)
    return (r + shift == c).astype(BF16)


def outward(step, count):
    half = lax.div(step + 1, 2)
    sign = 1 - 2 * lax.rem(step, 2)
    return lax.rem(count // 2 + half * sign + count, count)


def kernel(
    coef_in, member_in, kind_in, worth_in, start_in, shocks_in, bmap_in, cw,
    exp_out, coef_out, basis_out,
    coef, member, kind, worth, start, shocks, bmap, onehot, tsend, trecv, pk, bbuf, cwown, cwbuf, cown, fsend, call, net, gsend, gbuf,
    exsend, exbuf, qsend, qbuf, csend, cbuf, ssem, rsem, lsem,
):
    me_t = lax.axis_index("trade")
    me_p = lax.axis_index("path")
    x, y = lax.div(me_t, NY), lax.rem(me_t, NY)
    z, core = lax.div(me_p, 2), lax.rem(me_p, 2)
    date = lax.div(me_p, NP // 2)

    def trade_peer(step):
        dy = outward(lax.div(step, NT // NY), NY)
        dx = outward(lax.rem(step, NT // NY), NT // NY)
        return lax.rem(x + dx, NT // NY) * NY + lax.rem(y + dy, NY)

    def path_peer(step):
        dz = outward(lax.div(step, 2), NP // 2)
        dc = 1 - lax.rem(step, 2)
        return lax.rem(z + dz, NP // 2) * 2 + lax.rem(core + dc, 2)

    def put(src, dst, slot, dev):
        pltpu.make_async_remote_copy(
            src_ref=src, dst_ref=dst, send_sem=ssem.at[slot], recv_sem=rsem.at[slot],
            device_id=dev, device_id_type=MESH,
        ).start()

    def over_trade(src_of, dst, slot):
        def one(step, carry):
            peer = trade_peer(step)
            put(src_of(peer), dst.at[me_t], slot, (peer, me_p))
            return carry

        lax.fori_loop(0, NT - 1, one, 0)

    def over_path(src_of, dst, slot):
        def one(step, carry):
            peer = path_peer(step)
            put(src_of(peer), dst.at[me_p], slot, (me_t, peer))
            return carry

        lax.fori_loop(0, NP - 1, one, 0)

    def arrived(ref, slot):
        pltpu.make_async_copy(ref, ref, rsem.at[slot]).wait()

    def sent(ref, slot):
        pltpu.make_async_copy(ref, ref, ssem.at[slot]).wait()

    barrier = pltpu.get_barrier_semaphore()

    def greet_trade(step, carry):
        pl.semaphore_signal(barrier, inc=1, device_id=(trade_peer(step), me_p), device_id_type=MESH)
        return carry

    def greet_path(step, carry):
        pl.semaphore_signal(barrier, inc=1, device_id=(me_t, path_peer(step)), device_id_type=MESH)
        return carry

    lax.fori_loop(0, NT - 1, greet_trade, 0)
    lax.fori_loop(0, NP - 1, greet_path, 0)

    sets = pl.ds(pl.multiple_of(me_t * 128, 128), 128)
    loads = [
        pltpu.make_async_copy(src, dst, lsem.at[n])
        for n, (src, dst) in enumerate((
            (start_in, start), (shocks_in, shocks), (bmap_in, bmap), (kind_in, kind),
            (worth_in, worth), (member_in, member), (coef_in.at[2 * date + core], coef),
            (cw.at[:, :, sets], cwown),
        ))
    ]
    for load in loads:
        load.start()
    for load in loads[:-1]:
        load.wait()

    kinds = kind[...]
    notional = jnp.zeros(kinds.shape, F32)
    for n in range(8):
        notional = jnp.where(kinds == n, worth[0:1, n : n + 1], notional)
    eye64 = eye(64, 64, 0)
    left, right = eye(64, 128, 0), eye(64, 128, 64)
    start_t = dot_nt(eye64, start[...]).astype(BF16)
    later_t = jnp.tanh(dot(start_t, bmap[...]) + dot_nt(eye64, shocks[...])).astype(BF16)
    slope = 1.0 - dot_nt(eye64, later_t) ** 2
    bases = (start_t, later_t)

    def pack(v):
        return (dot(v[0:32], left) + dot(v[32:64], right)).astype(BF16)

    pk[0] = pack(start_t)
    pk[1] = pack(later_t)

    high, low = split(coef[...].astype(F32) * notional)
    both = jnp.concatenate([high, low], axis=0)
    members = member[...]

    def by_set(b, carry):
        ids = lax.broadcasted_iota(jnp.int32, (128, 512), 0) + b * 128
        hot = (members == ids).astype(F32).astype(BF16)
        onehot[b] = hot
        part = dot_nt(both, hot)
        tsend[b] = (part[0:32] + part[32:64]).astype(BF16)
        return carry

    lax.fori_loop(0, NT, by_set, 0, unroll=2)
    trecv[me_t] = tsend[me_t]

    pl.semaphore_wait(barrier, NT + NP - 2)
    over_trade(lambda peer: tsend.at[peer], trecv, 0)
    over_path(lambda peer: pk.at[lax.div(peer, NP // 2)], bbuf, 1)
    over_path(lambda peer: cw.at[lax.div(peer, NP // 2), :, sets], cwbuf, 2)
    loads[-1].wait()
    bbuf[me_p] = pk[date]
    cwbuf[me_p] = cwown[date]

    arrived(trecv.at[pl.ds(0, NT - 1)], 0)
    total = trecv[0].astype(F32)
    for n in range(1, NT):
        total = total + trecv[n].astype(F32)
    mine = 2 * date + core
    cown[core] = total
    fsend[...] = total.astype(BF16)
    far = lax.rem(z + NP // 4, NP // 2)
    put(cown.at[core], cown.at[core], 3, (me_t, 2 * z + 1 - core))
    put(fsend, call.at[mine], 4, (me_t, 2 * far + core))
    put(fsend, call.at[mine], 4, (me_t, 2 * far + 1 - core))

    arrived(bbuf.at[pl.ds(0, NP - 1)], 1)
    arrived(cwbuf.at[pl.ds(0, NP - 1)], 2)
    packed = bbuf[...].reshape(512, 128)
    q = lax.rem(me_p, NP // 2)
    r = lax.broadcasted_iota(jnp.int32, (16, 128), 0)
    c = lax.broadcasted_iota(jnp.int32, (16, 128), 1)
    want = jnp.where(r < 8, 8 * q + r, 56 + 8 * q + r)
    rows_b = dot_nt((c == want).astype(F32).astype(BF16), packed).astype(BF16)

    arrived(cown.at[0], 3)
    none = jnp.zeros((64, 128), BF16)
    weights = []
    for part in split(cown[...].reshape(64, 128)):
        weights.append(jnp.concatenate([part, none], axis=1))
        weights.append(jnp.concatenate([none, part], axis=1))
    call[pl.ds(2 * date, 2)] = cown[...].astype(BF16)
    netted = dot(jnp.concatenate([packed, packed], axis=1), jnp.concatenate(weights, axis=0))
    net[...] = netted
    cw_a = cwbuf[:, 0:32, :].reshape(512, 128).astype(F32)
    cw_b = cwbuf[:, 32:64, :].reshape(512, 128).astype(F32)
    adj_a = (cw_a * jax.nn.sigmoid(netted[:, 0:128])).astype(BF16)
    adj_b = (cw_b * jax.nn.sigmoid(netted[:, 128:256])).astype(BF16)
    grad = dot(rows_b[0:8], adj_a) + dot(rows_b[8:16], adj_b)
    gsend[...] = grad
    gbuf[me_t] = grad
    over_trade(lambda peer: gsend, gbuf, 5)

    wide = net[...]
    soft = jnp.maximum(wide, 0.0) + jnp.log1p(jnp.exp(-jnp.abs(wide)))
    soft = jnp.sum(soft, axis=0, keepdims=True)
    exposure = (soft[:, 0:128] + soft[:, 128:256]) / 1024.0
    exsend[...] = jnp.broadcast_to(exposure, (8, 128))
    put(exsend, exbuf, 6, (me_t, lax.rem(me_p + NP // 2, NP)))

    arrived(call.at[pl.ds(0, 2)], 4)
    pulls = []
    for t in range(2):
        c_t = call[2 * t : 2 * t + 2].reshape(64, 128)
        adj = (cwown[t].astype(F32) * jax.nn.sigmoid(dot(bases[t], c_t))).astype(BF16)
        pulls.append(dot_nt(c_t, adj))
    high, low = split(pulls[1] * slope)
    carried = dot(bmap[...], high) + dot(bmap[...], low)
    partial = pack(((pulls[0] + carried) / 128.0).astype(BF16))
    qsend[...] = partial
    qbuf[me_t] = partial
    over_trade(lambda peer: qsend, qbuf, 7)

    arrived(gbuf.at[pl.ds(0, NT - 1)], 5)
    rows = jnp.zeros((16, 512), F32)
    for n in range(0, NT, 4):
        part = jnp.concatenate([gbuf[n + m] for m in range(4)], axis=1)
        high, low = split(part)
        rows = rows + dot(
            jnp.concatenate([high, low], axis=0), onehot[n : n + 4].reshape(512, 512)
        )
    rows = (rows[0:8] + rows[8:16]) * (notional / 32.0)
    folded = jnp.concatenate([rows[:, 0:256], rows[:, 256:512]], axis=0).astype(BF16)
    csend[...] = folded
    cbuf[me_p] = folded
    over_path(lambda peer: csend, cbuf, 8)

    arrived(qbuf.at[pl.ds(0, NT - 1)], 7)
    total = qbuf[0].astype(F32)
    for n in range(1, NT):
        total = total + qbuf[n].astype(F32)
    basis_out[0:32, :] = total[:, 0:64]
    basis_out[32:64, :] = pltpu.roll(total, 64, 1)[:, 0:64]

    arrived(exbuf, 6)
    row = lax.broadcasted_iota(jnp.int32, (2, 128), 0)
    exp_out[...] = jnp.where(row == date, exsend[0:2, :], exbuf[0:2, :])

    arrived(cbuf.at[pl.ds(0, NP - 1)], 8)
    for n in range(NP):
        t, k = n // 8, 8 * (n % 8)
        block = cbuf[n].astype(F32)
        coef_out[t, k : k + 8, 0:256] = block[0:8]
        coef_out[t, k : k + 8, 256:512] = block[8:16]

    sent(trecv.at[pl.ds(0, NT - 1)], 0)
    sent(bbuf.at[pl.ds(0, NP - 1)], 1)
    sent(cwbuf.at[pl.ds(0, NP - 1)], 2)
    sent(cown.at[0], 3)
    sent(call.at[pl.ds(0, 2)], 4)
    sent(gbuf.at[pl.ds(0, NT - 1)], 5)
    sent(exbuf, 6)
    sent(qbuf.at[pl.ds(0, NT - 1)], 7)
    sent(cbuf.at[pl.ds(0, NP - 1)], 8)


def shards(
    coef, membership, trade_type, type_notional, basis_start, shocks, basis_map, credit_weight
):
    vmem = pl.BlockSpec(memory_space=pltpu.VMEM)
    hbm = pl.BlockSpec(memory_space=pltpu.HBM)
    return pl.pallas_call(
        kernel,
        out_shape=(
            jax.ShapeDtypeStruct((2, 128), F32),
            jax.ShapeDtypeStruct((2, 64, 512), F32),
            jax.ShapeDtypeStruct((64, 64), F32),
        ),
        in_specs=[hbm] * 8,
        out_specs=(vmem, vmem, vmem),
        scratch_shapes=[
            pltpu.VMEM((32, 512), BF16),
            pltpu.VMEM((1, 512), jnp.int32),
            pltpu.VMEM((1, 512), jnp.int32),
            pltpu.VMEM((1, 8), F32),
            pltpu.VMEM((64, 64), BF16),
            pltpu.VMEM((64, 64), BF16),
            pltpu.VMEM((64, 64), BF16),
            pltpu.VMEM((NT, 128, 512), BF16),
            pltpu.VMEM((NT, 32, 128), BF16),
            pltpu.VMEM((NT, 32, 128), BF16),
            pltpu.VMEM((2, 32, 128), BF16),
            pltpu.VMEM((NP, 32, 128), BF16),
            pltpu.VMEM((2, 64, 128), BF16),
            pltpu.VMEM((NP, 64, 128), BF16),
            pltpu.VMEM((2, 32, 128), F32),
            pltpu.VMEM((32, 128), BF16),
            pltpu.VMEM((4, 32, 128), BF16),
            pltpu.VMEM((512, 256), F32),
            pltpu.VMEM((8, 128), F32),
            pltpu.VMEM((NT, 8, 128), F32),
            pltpu.VMEM((8, 128), F32),
            pltpu.VMEM((8, 128), F32),
            pltpu.VMEM((32, 128), BF16),
            pltpu.VMEM((NT, 32, 128), BF16),
            pltpu.VMEM((16, 256), BF16),
            pltpu.VMEM((NP, 16, 256), BF16),
            pltpu.SemaphoreType.DMA((9,)),
            pltpu.SemaphoreType.DMA((9,)),
            pltpu.SemaphoreType.DMA((8,)),
        ],
        compiler_params=pltpu.CompilerParams(
            collective_id=0, has_side_effects=True, vmem_limit_bytes=40 * 2**20
        ),
    )(*(pltpu.with_memory_space_constraint(v, pltpu.HBM) for v in (
        coef.reshape(4, 32, 512), membership.reshape(1, 512), trade_type.reshape(1, 512),
        type_notional.reshape(1, 8), basis_start, shocks, basis_map, credit_weight,
    )))


def solution(mesh):
    placed = (
        P(None, None, "trade"),
        P("trade"),
        P("trade"),
        P(),
        P(None, "path"),
        P(None, "path"),
        P(),
        P(None, "path", None),
    )
    return jax.shard_map(
        shards,
        mesh=mesh,
        in_specs=placed,
        out_specs=(P(None, "trade"), P(None, None, "trade"), P(None, "path")),
        check_vma=False,
    )
```

time: 456 us -> 45.4 us (0.10)
  waiting for transfers between devices: 249 us -> 0 us
  blocking collectives: 169 us -> 0 us
  Pallas kernels: 0 us -> 42.7 us
  between operations: 14.2 us -> 0.64 us
  matrix products: 11.7 us -> 0 us
  other arithmetic: 6.7 us -> 0 us
    psum x2 -> x0, waiting for transfers between devices: 249 us -> none  [the longest x1 166 us: shards(): full = lax.psum((totals[0], totals[1]), 'trade')]
    psum x2 -> x0, blocking collectives: 169 us -> none  [the longest x1 113 us: shards(): early_pull = lax.psum(pulls[0], 'trade')]
    pallas_call x0 -> x1, Pallas kernels: none -> 42.7 us  [shards(): pl.pallas_call(kernel, out_shape=(jax.ShapeDtypeStruct((2, 128), F32), ja...]
    dot_general x16 -> x0, matrix products: 11.7 us -> none  [the longest x4 4.32 us: forward(): jnp.dot(lax.dynamic_slice_in_dim(values[step], start, block, 1), onehot,...]
  transfers between devices with their start and end apart: 2 -> 0, of which waited for: 2 -> 0; matrix products, arithmetic and copies ran while one was open for 0% -> 0% of each run, Pallas kernels for 0% -> 0%
where the time goes in v1:
time: 45.4 us; the launch traced here: 45.2 us
  Pallas kernels  42.7 us (94%)
  local copies, waits for them, and re-layouts  1.88 us (4%)
  between operations  0.64 us (1%)
    pallas_call x1, Pallas kernels, shards(): pl.pallas_call(kernel, out_shape=(jax.ShapeDtypeStruct((2, 128), F32), ja...  42.7 us
    unnamed x3, local copies, waits for them, and re-layouts  1.88 us

profile of v1, /device:TPU:1, one launch (start us, length us, event | category | flops | bytes accessed | tf_op | source)
XLA Modules:
  0.0 45.2 jit_solution(12452030481222161374)
XLA Ops:
  0.6 42.7 %shard_map.103 = (f32[2,128]{1,0:T(2,128)S(1)}, f32[2,64,512]{2,1,0:T(8,128)S(1)}, f32[64,64]{1,0:T(8,128)S(1)}) custom-call(bf16[4,32,512]{2,1,0:T(8,128)(2,1)} %bitcast.4, s32[1,512]{1,0:T(1,128)} %bitcast.5, s32[1,512]{1,0:T(1,128)} %bitcast.6, f32[1,8]{1,0:T(1,128)} %bitcast.7, bf16[64,64]{1,0:T(8,128)(2,1)} %start_in.1, bf16[64,64]{1,0:T(8,128)(2,1)} %shocks_in.1, ...), custom_call_target="tpu_custom_call" | custom-call | tf_op jit(solution)/shard_map/pallas_call | solution.py:268
  43.3 0.6 %copy.14 = f32[2,128]{1,0:T(2,128)} copy(f32[2,128]{1,0:T(2,128)S(1)} %get-tuple-element.6) | data formatting | bytes 2048
  43.9 0.7 %copy.15 = f32[2,64,512]{2,1,0:T(8,128)} copy(f32[2,64,512]{2,1,0:T(8,128)S(1)} %get-tuple-element.7) | data formatting | bytes 524288
  44.6 0.6 %copy.16 = f32[64,64]{1,0:T(8,128)} copy(f32[64,64]{1,0:T(8,128)S(1)} %get-tuple-element.8) | data formatting | bytes 32768

commit v2 on v1

--- a/solution.py
+++ b/solution.py
@@ -35,16 +35,24 @@
     return (r + shift == c).astype(BF16)
 
 
-def outward(step, count):
-    half = lax.div(step + 1, 2)
-    sign = 1 - 2 * lax.rem(step, 2)
-    return lax.rem(count // 2 + half * sign + count, count)
+def hops(offset, count):
+    return min(offset, count - offset)
+
+
+def farthest_first(offsets, counts):
+    return sorted(offsets, key=lambda o: -sum(hops(v, n) for v, n in zip(o, counts)))
+
+
+NX = NT // NY
+NZ = NP // 2
+TRADE_PEERS = farthest_first([(a, b) for a in range(NX) for b in range(NY)], (NX, NY))[:-1]
+PATH_PEERS = farthest_first([(a, b) for a in range(NZ) for b in range(2)], (NZ, 2))[:-1]
 
 
 def kernel(
     coef_in, member_in, kind_in, worth_in, start_in, shocks_in, bmap_in, cw,
     exp_out, coef_out, basis_out,
-    coef, member, kind, worth, start, shocks, bmap, onehot, tsend, trecv, pk, bbuf, cwown, cwbuf, cown, fsend, call, net, gsend, gbuf,
+    coef, member, kind, worth, start, shocks, bmap, onehot, tsend, trecv, psend, pbuf, cown, fsend, call, net, gsend, gbuf,
     exsend, exbuf, qsend, qbuf, csend, cbuf, ssem, rsem, lsem,
 ):
     me_t = lax.axis_index("trade")
@@ -53,15 +61,12 @@
     z, core = lax.div(me_p, 2), lax.rem(me_p, 2)
     date = lax.div(me_p, NP // 2)
 
-    def trade_peer(step):
-        dy = outward(lax.div(step, NT // NY), NY)
-        dx = outward(lax.rem(step, NT // NY), NT // NY)
-        return lax.rem(x + dx, NT // NY) * NY + lax.rem(y + dy, NY)
-
-    def path_peer(step):
-        dz = outward(lax.div(step, 2), NP // 2)
-        dc = 1 - lax.rem(step, 2)
-        return lax.rem(z + dz, NP // 2) * 2 + lax.rem(core + dc, 2)
+    xs = [lax.rem(x + n, NX) * NY for n in range(NX)]
+    ys = [lax.rem(y + n, NY) for n in range(NY)]
+    zs = [lax.rem(z + n, NZ) for n in range(NZ)]
+    cores = [core, 1 - core]
+    trade_peers = [xs[a] + ys[b] for a, b in TRADE_PEERS]
+    path_peers = [2 * zs[a] + cores[b] for a, b in PATH_PEERS]
 
     def put(src, dst, slot, dev):
         pltpu.make_async_remote_copy(
@@ -70,20 +75,12 @@
         ).start()
 
     def over_trade(src_of, dst, slot):
-        def one(step, carry):
-            peer = trade_peer(step)
+        for peer in trade_peers:
             put(src_of(peer), dst.at[me_t], slot, (peer, me_p))
-            return carry
-
-        lax.fori_loop(0, NT - 1, one, 0)
 
     def over_path(src_of, dst, slot):
-        def one(step, carry):
-            peer = path_peer(step)
+        for peer in path_peers:
             put(src_of(peer), dst.at[me_p], slot, (me_t, peer))
-            return carry
-
-        lax.fori_loop(0, NP - 1, one, 0)
 
     def arrived(ref, slot):
         pltpu.make_async_copy(ref, ref, rsem.at[slot]).wait()
@@ -93,16 +90,10 @@
 
     barrier = pltpu.get_barrier_semaphore()
 
-    def greet_trade(step, carry):
-        pl.semaphore_signal(barrier, inc=1, device_id=(trade_peer(step), me_p), device_id_type=MESH)
-        return carry
-
-    def greet_path(step, carry):
-        pl.semaphore_signal(barrier, inc=1, device_id=(me_t, path_peer(step)), device_id_type=MESH)
-        return carry
-
-    lax.fori_loop(0, NT - 1, greet_trade, 0)
-    lax.fori_loop(0, NP - 1, greet_path, 0)
+    for peer in trade_peers:
+        pl.semaphore_signal(barrier, inc=1, device_id=(peer, me_p), device_id_type=MESH)
+    for peer in path_peers:
+        pl.semaphore_signal(barrier, inc=1, device_id=(me_t, peer), device_id_type=MESH)
 
     sets = pl.ds(pl.multiple_of(me_t * 128, 128), 128)
     loads = [
@@ -110,12 +101,12 @@
         for n, (src, dst) in enumerate((
             (start_in, start), (shocks_in, shocks), (bmap_in, bmap), (kind_in, kind),
             (worth_in, worth), (member_in, member), (coef_in.at[2 * date + core], coef),
-            (cw.at[:, :, sets], cwown),
+            (cw.at[:, :, sets], psend.at[:, 0:64, :]),
         ))
     ]
     for load in loads:
         load.start()
-    for load in loads[:-1]:
+    for load in loads:
         load.wait()
 
     kinds = kind[...]
@@ -132,8 +123,9 @@
     def pack(v):
         return (dot(v[0:32], left) + dot(v[32:64], right)).astype(BF16)
 
-    pk[0] = pack(start_t)
-    pk[1] = pack(later_t)
+    psend[0, 64:96, :] = pack(start_t)
+    psend[1, 64:96, :] = pack(later_t)
+    pbuf[core, z] = psend[date]
 
     high, low = split(coef[...].astype(F32) * notional)
     both = jnp.concatenate([high, low], axis=0)
@@ -151,12 +143,12 @@
     trecv[me_t] = tsend[me_t]
 
     pl.semaphore_wait(barrier, NT + NP - 2)
+    for n in (4, 3, 5, 2, 6, 1, 7):
+        put(psend.at[lax.div(zs[n], NZ // 2)], pbuf.at[core, z], 1, (me_t, 2 * zs[n] + core))
     over_trade(lambda peer: tsend.at[peer], trecv, 0)
-    over_path(lambda peer: pk.at[lax.div(peer, NP // 2)], bbuf, 1)
-    over_path(lambda peer: cw.at[lax.div(peer, NP // 2), :, sets], cwbuf, 2)
-    loads[-1].wait()
-    bbuf[me_p] = pk[date]
-    cwbuf[me_p] = cwown[date]
+
+    arrived(pbuf.at[0, pl.ds(0, NZ - 1)], 1)
+    put(pbuf.at[core], pbuf.at[core], 2, (me_t, 2 * z + 1 - core))
 
     arrived(trecv.at[pl.ds(0, NT - 1)], 0)
     total = trecv[0].astype(F32)
@@ -165,14 +157,13 @@
     mine = 2 * date + core
     cown[core] = total
     fsend[...] = total.astype(BF16)
-    far = lax.rem(z + NP // 4, NP // 2)
+    far = zs[NZ // 2]
     put(cown.at[core], cown.at[core], 3, (me_t, 2 * z + 1 - core))
     put(fsend, call.at[mine], 4, (me_t, 2 * far + core))
     put(fsend, call.at[mine], 4, (me_t, 2 * far + 1 - core))
 
-    arrived(bbuf.at[pl.ds(0, NP - 1)], 1)
-    arrived(cwbuf.at[pl.ds(0, NP - 1)], 2)
-    packed = bbuf[...].reshape(512, 128)
+    arrived(pbuf.at[0], 2)
+    packed = pbuf[:, :, 64:96, :].reshape(512, 128)
     q = lax.rem(me_p, NP // 2)
     r = lax.broadcasted_iota(jnp.int32, (16, 128), 0)
     c = lax.broadcasted_iota(jnp.int32, (16, 128), 1)
@@ -188,8 +179,8 @@
     call[pl.ds(2 * date, 2)] = cown[...].astype(BF16)
     netted = dot(jnp.concatenate([packed, packed], axis=1), jnp.concatenate(weights, axis=0))
     net[...] = netted
-    cw_a = cwbuf[:, 0:32, :].reshape(512, 128).astype(F32)
-    cw_b = cwbuf[:, 32:64, :].reshape(512, 128).astype(F32)
+    cw_a = pbuf[:, :, 0:32, :].reshape(512, 128).astype(F32)
+    cw_b = pbuf[:, :, 32:64, :].reshape(512, 128).astype(F32)
     adj_a = (cw_a * jax.nn.sigmoid(netted[:, 0:128])).astype(BF16)
     adj_b = (cw_b * jax.nn.sigmoid(netted[:, 128:256])).astype(BF16)
     grad = dot(rows_b[0:8], adj_a) + dot(rows_b[8:16], adj_b)
@@ -208,7 +199,7 @@
     pulls = []
     for t in range(2):
         c_t = call[2 * t : 2 * t + 2].reshape(64, 128)
-        adj = (cwown[t].astype(F32) * jax.nn.sigmoid(dot(bases[t], c_t))).astype(BF16)
+        adj = (psend[t, 0:64, :].astype(F32) * jax.nn.sigmoid(dot(bases[t], c_t))).astype(BF16)
         pulls.append(dot_nt(c_t, adj))
     high, low = split(pulls[1] * slope)
     carried = dot(bmap[...], high) + dot(bmap[...], low)
@@ -250,8 +241,8 @@
         coef_out[t, k : k + 8, 256:512] = block[8:16]
 
     sent(trecv.at[pl.ds(0, NT - 1)], 0)
-    sent(bbuf.at[pl.ds(0, NP - 1)], 1)
-    sent(cwbuf.at[pl.ds(0, NP - 1)], 2)
+    sent(pbuf.at[0, pl.ds(0, NZ - 1)], 1)
+    sent(pbuf.at[0], 2)
     sent(cown.at[0], 3)
     sent(call.at[pl.ds(0, 2)], 4)
     sent(gbuf.at[pl.ds(0, NT - 1)], 5)
@@ -285,10 +276,8 @@
             pltpu.VMEM((NT, 128, 512), BF16),
             pltpu.VMEM((NT, 32, 128), BF16),
             pltpu.VMEM((NT, 32, 128), BF16),
-            pltpu.VMEM((2, 32, 128), BF16),
-            pltpu.VMEM((NP, 32, 128), BF16),
-            pltpu.VMEM((2, 64, 128), BF16),
-            pltpu.VMEM((NP, 64, 128), BF16),
+            pltpu.VMEM((2, 96, 128), BF16),
+            pltpu.VMEM((2, NP // 2, 96, 128), BF16),
             pltpu.VMEM((2, 32, 128), F32),
             pltpu.VMEM((32, 128), BF16),
             pltpu.VMEM((4, 32, 128), BF16),

time: 45.4 us -> 43.2 us (0.952)
  Pallas kernels: 42.7 us -> 40.5 us
    pallas_call x1, Pallas kernels: 42.7 us -> 40.5 us  [shards(): pl.pallas_call(kernel, out_shape=(jax.ShapeDtypeStruct((2, 128), F32), ja...]
where the time goes in v2:
time: 43.2 us; the launch traced here: 43 us
  Pallas kernels  40.5 us (94%)
  local copies, waits for them, and re-layouts  1.88 us (4%)
  between operations  0.64 us (1%)
    pallas_call x1, Pallas kernels, shards(): pl.pallas_call(kernel, out_shape=(jax.ShapeDtypeStruct((2, 128), F32), ja...  40.5 us
    unnamed x3, local copies, waits for them, and re-layouts  1.88 us

profile of v2, /device:TPU:1, one launch (start us, length us, event | category | flops | bytes accessed | tf_op | source)
XLA Modules:
  0.0 43.0 jit_solution(2320189550402030650)
XLA Ops:
  0.6 40.5 %shard_map.103 = (f32[2,128]{1,0:T(2,128)S(1)}, f32[2,64,512]{2,1,0:T(8,128)S(1)}, f32[64,64]{1,0:T(8,128)S(1)}) custom-call(bf16[4,32,512]{2,1,0:T(8,128)(2,1)} %bitcast.4, s32[1,512]{1,0:T(1,128)} %bitcast.5, s32[1,512]{1,0:T(1,128)} %bitcast.6, f32[1,8]{1,0:T(1,128)} %bitcast.7, bf16[64,64]{1,0:T(8,128)(2,1)} %start_in.1, bf16[64,64]{1,0:T(8,128)(2,1)} %shocks_in.1, ...), custom_call_target="tpu_custom_call" | custom-call | tf_op jit(solution)/shard_map/pallas_call | solution.py:259
  41.2 0.6 %copy.14 = f32[2,128]{1,0:T(2,128)} copy(f32[2,128]{1,0:T(2,128)S(1)} %get-tuple-element.6) | data formatting | bytes 2048
  41.7 0.7 %copy.15 = f32[2,64,512]{2,1,0:T(8,128)} copy(f32[2,64,512]{2,1,0:T(8,128)S(1)} %get-tuple-element.7) | data formatting | bytes 524288
  42.4 0.6 %copy.16 = f32[64,64]{1,0:T(8,128)} copy(f32[64,64]{1,0:T(8,128)S(1)} %get-tuple-element.8) | data formatting | bytes 32768

commit v3 on v2

--- a/solution.py
+++ b/solution.py
@@ -106,27 +106,13 @@
     ]
     for load in loads:
         load.start()
-    for load in loads:
+    for load in loads[3:7]:
         load.wait()
 
     kinds = kind[...]
     notional = jnp.zeros(kinds.shape, F32)
     for n in range(8):
         notional = jnp.where(kinds == n, worth[0:1, n : n + 1], notional)
-    eye64 = eye(64, 64, 0)
-    left, right = eye(64, 128, 0), eye(64, 128, 64)
-    start_t = dot_nt(eye64, start[...]).astype(BF16)
-    later_t = jnp.tanh(dot(start_t, bmap[...]) + dot_nt(eye64, shocks[...])).astype(BF16)
-    slope = 1.0 - dot_nt(eye64, later_t) ** 2
-    bases = (start_t, later_t)
-
-    def pack(v):
-        return (dot(v[0:32], left) + dot(v[32:64], right)).astype(BF16)
-
-    psend[0, 64:96, :] = pack(start_t)
-    psend[1, 64:96, :] = pack(later_t)
-    pbuf[core, z] = psend[date]
-
     high, low = split(coef[...].astype(F32) * notional)
     both = jnp.concatenate([high, low], axis=0)
     members = member[...]
@@ -143,9 +129,26 @@
     trecv[me_t] = tsend[me_t]
 
     pl.semaphore_wait(barrier, NT + NP - 2)
+    over_trade(lambda peer: tsend.at[peer], trecv, 0)
+
+    for load in loads[:3] + loads[7:]:
+        load.wait()
+    eye64 = eye(64, 64, 0)
+    left, right = eye(64, 128, 0), eye(64, 128, 64)
+    start_t = dot_nt(eye64, start[...]).astype(BF16)
+    later_t = jnp.tanh(dot(start_t, bmap[...]) + dot_nt(eye64, shocks[...])).astype(BF16)
+    slope = 1.0 - dot_nt(eye64, later_t) ** 2
+    bases = (start_t, later_t)
+
+    def pack(v):
+        return (dot(v[0:32], left) + dot(v[32:64], right)).astype(BF16)
+
+    psend[0, 64:96, :] = pack(start_t)
+    psend[1, 64:96, :] = pack(later_t)
+    pbuf[core, z] = psend[date]
+
     for n in (4, 3, 5, 2, 6, 1, 7):
         put(psend.at[lax.div(zs[n], NZ // 2)], pbuf.at[core, z], 1, (me_t, 2 * zs[n] + core))
-    over_trade(lambda peer: tsend.at[peer], trecv, 0)
 
     arrived(pbuf.at[0, pl.ds(0, NZ - 1)], 1)
     put(pbuf.at[core], pbuf.at[core], 2, (me_t, 2 * z + 1 - core))
@@ -251,18 +254,32 @@
     sent(cbuf.at[pl.ds(0, NP - 1)], 8)
 
 
+def deliver(exp_in, coef_in, basis_in, exp_out, coef_out, basis_out, sems):
+    copies = [
+        pltpu.make_async_copy(src, dst, sems.at[n])
+        for n, (src, dst) in enumerate(
+            ((coef_in, coef_out), (basis_in, basis_out), (exp_in, exp_out))
+        )
+    ]
+    for copy in copies:
+        copy.start()
+    for copy in copies:
+        copy.wait()
+
+
 def shards(
     coef, membership, trade_type, type_notional, basis_start, shocks, basis_map, credit_weight
 ):
     vmem = pl.BlockSpec(memory_space=pltpu.VMEM)
     hbm = pl.BlockSpec(memory_space=pltpu.HBM)
-    return pl.pallas_call(
+    outs = (
+        jax.ShapeDtypeStruct((2, 128), F32),
+        jax.ShapeDtypeStruct((2, 64, 512), F32),
+        jax.ShapeDtypeStruct((64, 64), F32),
+    )
+    results = pl.pallas_call(
         kernel,
-        out_shape=(
-            jax.ShapeDtypeStruct((2, 128), F32),
-            jax.ShapeDtypeStruct((2, 64, 512), F32),
-            jax.ShapeDtypeStruct((64, 64), F32),
-        ),
+        out_shape=outs,
         in_specs=[hbm] * 8,
         out_specs=(vmem, vmem, vmem),
         scratch_shapes=[
@@ -301,6 +318,13 @@
         coef.reshape(4, 32, 512), membership.reshape(1, 512), trade_type.reshape(1, 512),
         type_notional.reshape(1, 8), basis_start, shocks, basis_map, credit_weight,
     )))
+    return pl.pallas_call(
+        deliver,
+        out_shape=outs,
+        in_specs=[vmem] * 3,
+        out_specs=(hbm,) * 3,
+        scratch_shapes=[pltpu.SemaphoreType.DMA((3,))],
+    )(*(pltpu.with_memory_space_constraint(v, pltpu.VMEM) for v in results))
 
 
 def solution(mesh):

time: 43.2 us -> 41.4 us (0.958)
  local copies, waits for them, and re-layouts: 1.88 us -> 0 us
    unnamed x3 -> x0, local copies, waits for them, and re-layouts: 1.88 us -> none
    pallas_call x1 -> x2, Pallas kernels: 40.5 us -> 40.6 us  [the longest x1 39.8 us: shards(): pl.pallas_call(kernel, out_shape=outs, in_specs=[hbm] * 8, out_specs=(vme...]
where the time goes in v3:
time: 41.4 us; the launch traced here: 41.2 us
  Pallas kernels  40.6 us (98%)
  between operations  0.64 us (2%)
    pallas_call x1, Pallas kernels, shards(): pl.pallas_call(kernel, out_shape=outs, in_specs=[hbm] * 8, out_specs=(vme...  39.8 us

profile of v3, /device:TPU:1, one launch (start us, length us, event | category | flops | bytes accessed | tf_op | source)
XLA Modules:
  0.0 41.2 jit_solution(15430312762760937968)
XLA Ops:
  0.6 39.8 %shard_map.103 = (f32[2,128]{1,0:T(2,128)S(1)}, f32[2,64,512]{2,1,0:T(8,128)S(1)}, f32[64,64]{1,0:T(8,128)S(1)}) custom-call(bf16[4,32,512]{2,1,0:T(8,128)(2,1)} %bitcast.4, s32[1,512]{1,0:T(1,128)} %bitcast.5, s32[1,512]{1,0:T(1,128)} %bitcast.6, f32[1,8]{1,0:T(1,128)} %bitcast.7, bf16[64,64]{1,0:T(8,128)(2,1)} %start_in.1, bf16[64,64]{1,0:T(8,128)(2,1)} %shocks_in.1, ...), custom_call_target="tpu_custom_call" | custom-call | tf_op jit(solution)/shard_map/pallas_call | solution.py:280
  40.5 0.7 %shard_map.104 = (f32[2,128]{1,0:T(2,128)}, f32[2,64,512]{2,1,0:T(8,128)}, f32[64,64]{1,0:T(8,128)}) custom-call(f32[2,128]{1,0:T(2,128)S(1)} %get-tuple-element.6.exp_in, f32[2,64,512]{2,1,0:T(8,128)S(1)} %get-tuple-element.7.coef_in, f32[64,64]{1,0:T(8,128)S(1)} %get-tuple-element.8.basis_in), custom_call_target="tpu_custom_call" | custom-call | tf_op jit(solution)/shard_map/pallas_call | solution.py:321

commit v4 on v3

--- a/solution.py
+++ b/solution.py
@@ -92,9 +92,6 @@
 
     for peer in trade_peers:
         pl.semaphore_signal(barrier, inc=1, device_id=(peer, me_p), device_id_type=MESH)
-    for peer in path_peers:
-        pl.semaphore_signal(barrier, inc=1, device_id=(me_t, peer), device_id_type=MESH)
-
     sets = pl.ds(pl.multiple_of(me_t * 128, 128), 128)
     loads = [
         pltpu.make_async_copy(src, dst, lsem.at[n])
@@ -106,6 +103,9 @@
     ]
     for load in loads:
         load.start()
+    for peer in path_peers:
+        pl.semaphore_signal(barrier, inc=1, device_id=(me_t, peer), device_id_type=MESH)
+
     for load in loads[3:7]:
         load.wait()
 
@@ -187,8 +187,8 @@
     adj_a = (cw_a * jax.nn.sigmoid(netted[:, 0:128])).astype(BF16)
     adj_b = (cw_b * jax.nn.sigmoid(netted[:, 128:256])).astype(BF16)
     grad = dot(rows_b[0:8], adj_a) + dot(rows_b[8:16], adj_b)
-    gsend[...] = grad
-    gbuf[me_t] = grad
+    gsend[...] = grad.astype(BF16)
+    gbuf[me_t] = grad.astype(BF16)
     over_trade(lambda peer: gsend, gbuf, 5)
 
     wide = net[...]
@@ -212,14 +212,10 @@
     over_trade(lambda peer: qsend, qbuf, 7)
 
     arrived(gbuf.at[pl.ds(0, NT - 1)], 5)
-    rows = jnp.zeros((16, 512), F32)
+    rows = jnp.zeros((8, 512), F32)
     for n in range(0, NT, 4):
         part = jnp.concatenate([gbuf[n + m] for m in range(4)], axis=1)
-        high, low = split(part)
-        rows = rows + dot(
-            jnp.concatenate([high, low], axis=0), onehot[n : n + 4].reshape(512, 512)
-        )
-    rows = (rows[0:8] + rows[8:16]) * (notional / 32.0)
+        rows = rows + dot(part, onehot[n : n + 4].reshape(512, 512))
     folded = jnp.concatenate([rows[:, 0:256], rows[:, 256:512]], axis=0).astype(BF16)
     csend[...] = folded
     cbuf[me_p] = folded
@@ -237,11 +233,12 @@
     exp_out[...] = jnp.where(row == date, exsend[0:2, :], exbuf[0:2, :])
 
     arrived(cbuf.at[pl.ds(0, NP - 1)], 8)
+    scale = notional / 32.0
     for n in range(NP):
         t, k = n // 8, 8 * (n % 8)
         block = cbuf[n].astype(F32)
-        coef_out[t, k : k + 8, 0:256] = block[0:8]
-        coef_out[t, k : k + 8, 256:512] = block[8:16]
+        coef_out[t, k : k + 8, 0:256] = block[0:8] * scale[:, 0:256]
+        coef_out[t, k : k + 8, 256:512] = block[8:16] * scale[:, 256:512]
 
     sent(trecv.at[pl.ds(0, NT - 1)], 0)
     sent(pbuf.at[0, pl.ds(0, NZ - 1)], 1)
@@ -299,8 +296,8 @@
             pltpu.VMEM((32, 128), BF16),
             pltpu.VMEM((4, 32, 128), BF16),
             pltpu.VMEM((512, 256), F32),
-            pltpu.VMEM((8, 128), F32),
-            pltpu.VMEM((NT, 8, 128), F32),
+            pltpu.VMEM((8, 128), BF16),
+            pltpu.VMEM((NT, 8, 128), BF16),
             pltpu.VMEM((8, 128), F32),
             pltpu.VMEM((8, 128), F32),
             pltpu.VMEM((32, 128), BF16),

time: 41.4 us -> 40.2 us (0.971)
  Pallas kernels: 40.6 us -> 39.4 us
    pallas_call x1, Pallas kernels: 39.8 us -> 38.7 us  [shards(): pl.pallas_call(kernel, out_shape=outs, in_specs=[hbm] * 8, out_specs=(vme...]
where the time goes in v4:
time: 40.2 us; the launch traced here: 40 us
  Pallas kernels  39.4 us (98%)
  between operations  0.64 us (2%)
    pallas_call x1, Pallas kernels, shards(): pl.pallas_call(kernel, out_shape=outs, in_specs=[hbm] * 8, out_specs=(vme...  38.7 us

profile of v4, /device:TPU:1, one launch (start us, length us, event | category | flops | bytes accessed | tf_op | source)
XLA Modules:
  0.0 40.0 jit_solution(11348608469175267737)
XLA Ops:
  0.6 38.7 %shard_map.103 = (f32[2,128]{1,0:T(2,128)S(1)}, f32[2,64,512]{2,1,0:T(8,128)S(1)}, f32[64,64]{1,0:T(8,128)S(1)}) custom-call(bf16[4,32,512]{2,1,0:T(8,128)(2,1)} %bitcast.4, s32[1,512]{1,0:T(1,128)} %bitcast.5, s32[1,512]{1,0:T(1,128)} %bitcast.6, f32[1,8]{1,0:T(1,128)} %bitcast.7, bf16[64,64]{1,0:T(8,128)(2,1)} %start_in.1, bf16[64,64]{1,0:T(8,128)(2,1)} %shocks_in.1, ...), custom_call_target="tpu_custom_call" | custom-call | tf_op jit(solution)/shard_map/pallas_call | solution.py:277
  39.3 0.7 %shard_map.104 = (f32[2,128]{1,0:T(2,128)}, f32[2,64,512]{2,1,0:T(8,128)}, f32[64,64]{1,0:T(8,128)}) custom-call(f32[2,128]{1,0:T(2,128)S(1)} %get-tuple-element.6.exp_in, f32[2,64,512]{2,1,0:T(8,128)S(1)} %get-tuple-element.7.coef_in, f32[64,64]{1,0:T(8,128)S(1)} %get-tuple-element.8.basis_in), custom_call_target="tpu_custom_call" | custom-call | tf_op jit(solution)/shard_map/pallas_call | solution.py:318

commit v5 on v4

--- a/solution.py
+++ b/solution.py
@@ -77,10 +77,6 @@
     def over_trade(src_of, dst, slot):
         for peer in trade_peers:
             put(src_of(peer), dst.at[me_t], slot, (peer, me_p))
-
-    def over_path(src_of, dst, slot):
-        for peer in path_peers:
-            put(src_of(peer), dst.at[me_p], slot, (me_t, peer))
 
     def arrived(ref, slot):
         pltpu.make_async_copy(ref, ref, rsem.at[slot]).wait()
@@ -218,8 +214,12 @@
         rows = rows + dot(part, onehot[n : n + 4].reshape(512, 512))
     folded = jnp.concatenate([rows[:, 0:256], rows[:, 256:512]], axis=0).astype(BF16)
     csend[...] = folded
-    cbuf[me_p] = folded
-    over_path(lambda peer: csend, cbuf, 8)
+    cbuf[core, z] = folded
+    for n in (4, 3, 5, 2, 6, 1, 7):
+        put(csend, cbuf.at[core, z], 8, (me_t, 2 * zs[n] + core))
+
+    arrived(cbuf.at[0, pl.ds(0, NZ - 1)], 8)
+    put(cbuf.at[core], cbuf.at[core], 9, (me_t, 2 * z + 1 - core))
 
     arrived(qbuf.at[pl.ds(0, NT - 1)], 7)
     total = qbuf[0].astype(F32)
@@ -232,13 +232,15 @@
     row = lax.broadcasted_iota(jnp.int32, (2, 128), 0)
     exp_out[...] = jnp.where(row == date, exsend[0:2, :], exbuf[0:2, :])
 
-    arrived(cbuf.at[pl.ds(0, NP - 1)], 8)
     scale = notional / 32.0
-    for n in range(NP):
-        t, k = n // 8, 8 * (n % 8)
-        block = cbuf[n].astype(F32)
-        coef_out[t, k : k + 8, 0:256] = block[0:8] * scale[:, 0:256]
-        coef_out[t, k : k + 8, 256:512] = block[8:16] * scale[:, 256:512]
+    for side in cores:
+        if side is not core:
+            arrived(cbuf.at[0], 9)
+        for n in range(NZ):
+            k = pl.ds(pl.multiple_of(8 * (2 * (n % 4) + side), 8), 8)
+            block = cbuf[side, n].astype(F32)
+            coef_out[n // 4, k, 0:256] = block[0:8] * scale[:, 0:256]
+            coef_out[n // 4, k, 256:512] = block[8:16] * scale[:, 256:512]
 
     sent(trecv.at[pl.ds(0, NT - 1)], 0)
     sent(pbuf.at[0, pl.ds(0, NZ - 1)], 1)
@@ -248,7 +250,8 @@
     sent(gbuf.at[pl.ds(0, NT - 1)], 5)
     sent(exbuf, 6)
     sent(qbuf.at[pl.ds(0, NT - 1)], 7)
-    sent(cbuf.at[pl.ds(0, NP - 1)], 8)
+    sent(cbuf.at[0, pl.ds(0, NZ - 1)], 8)
+    sent(cbuf.at[0], 9)
 
 
 def deliver(exp_in, coef_in, basis_in, exp_out, coef_out, basis_out, sems):
@@ -303,9 +306,9 @@
             pltpu.VMEM((32, 128), BF16),
             pltpu.VMEM((NT, 32, 128), BF16),
             pltpu.VMEM((16, 256), BF16),
-            pltpu.VMEM((NP, 16, 256), BF16),
-            pltpu.SemaphoreType.DMA((9,)),
-            pltpu.SemaphoreType.DMA((9,)),
+            pltpu.VMEM((2, NP // 2, 16, 256), BF16),
+            pltpu.SemaphoreType.DMA((10,)),
+            pltpu.SemaphoreType.DMA((10,)),
             pltpu.SemaphoreType.DMA((8,)),
         ],
         compiler_params=pltpu.CompilerParams(

time: 40.2 us -> 40.3 us (level)
  no operation moved by 1% of the time
where the time goes in v5:
time: 40.3 us; the launch traced here: 40.1 us
  Pallas kernels  39.4 us (98%)
  between operations  0.64 us (2%)
    pallas_call x1, Pallas kernels, shards(): pl.pallas_call(kernel, out_shape=outs, in_specs=[hbm] * 8, out_specs=(vme...  38.7 us

profile of v5, /device:TPU:1, one launch (start us, length us, event | category | flops | bytes accessed | tf_op | source)
XLA Modules:
  0.0 40.1 jit_solution(13909242497743646267)
XLA Ops:
  0.6 38.7 %shard_map.103 = (f32[2,128]{1,0:T(2,128)S(1)}, f32[2,64,512]{2,1,0:T(8,128)S(1)}, f32[64,64]{1,0:T(8,128)S(1)}) custom-call(bf16[4,32,512]{2,1,0:T(8,128)(2,1)} %bitcast.4, s32[1,512]{1,0:T(1,128)} %bitcast.5, s32[1,512]{1,0:T(1,128)} %bitcast.6, f32[1,8]{1,0:T(1,128)} %bitcast.7, bf16[64,64]{1,0:T(8,128)(2,1)} %start_in.1, bf16[64,64]{1,0:T(8,128)(2,1)} %shocks_in.1, ...), custom_call_target="tpu_custom_call" | custom-call | tf_op jit(solution)/shard_map/pallas_call | solution.py:280
  39.3 0.7 %shard_map.104 = (f32[2,128]{1,0:T(2,128)}, f32[2,64,512]{2,1,0:T(8,128)}, f32[64,64]{1,0:T(8,128)}) custom-call(f32[2,128]{1,0:T(2,128)S(1)} %get-tuple-element.6.exp_in, f32[2,64,512]{2,1,0:T(8,128)S(1)} %get-tuple-element.7.coef_in, f32[64,64]{1,0:T(8,128)S(1)} %get-tuple-element.8.basis_in), custom_call_target="tpu_custom_call" | custom-call | tf_op jit(solution)/shard_map/pallas_call | solution.py:321
